TPU v7x, 32 devices: a whole 2x2x4 slice. The times are simulated.
32 devices in a mesh: blk: 8 (over y, x, core), path: 4 (over z).
Axes of the slice: x: 2, y: 2, z: 4, core: 2. Of those that a mesh axis runs over, the one named last changes fastest.
Arguments:
- records: bfloat16 [8192, 512], P('blk'), may hold values from -87.98545 to 87.98545
- coefficients: float32 [8192, 64], P('blk', 'path'), may hold values from -6 to 6
- velocity: float32 [8192, 64], P('blk', 'path'), may hold values from -3 to 3
- targets: float32 [8192, 64], P('blk', 'path'), may hold values from -6 to 6
- block_local: int32 [3, 192], P(None, 'blk'), may hold values from 0 to 1023
- block_count: int32 [3, 8], replicated, may hold values from 1 to 24, 128 in all within a row
- candidates: bfloat16 [4096, 512], P('blk'), may hold values from -87.98545 to 87.98545
- frequencies: bfloat16 [512, 1024], replicated, may hold values from -0.25 to 0.25
- phases: float32 [1024], replicated, may hold values from -3.140625 to 3.140625
- prior_weight: float32 [1024, 64], P(None, 'path'), may hold values from -6 to 6
Outputs:
- coefficients_out: float32 [8192, 64], P('blk', 'path')
- velocity_out: float32 [8192, 64], P('blk', 'path')
- scores: float32 [4096, 64], P('blk', 'path')
- path_rms: float32 [4096], P('blk')
Inputs may be any that keep to these rules, and one draw needn't show every extreme that they name: `block_count`: each row sums to 128, and its largest entry is exactly 24. `block_local`: index within the owner's records; a slot at or beyond the owner's count in that step is not used. Used entries of one owner may repeat.
All inputs are finite; a program needn't handle non-finite values.
Results may differ from a plain program's by a relative error of at most 0.0014.
Values may be sent and summed in bfloat16 or wider, within the bound.
A program may use at most 128 MiB of HBM per device.

v0:
```python
import functools
import math

import jax
import jax.numpy as jnp
from jax import lax
from jax.experimental import pallas as pl
from jax.experimental.pallas import tpu as pltpu
from jax.sharding import PartitionSpec as P

NOISE = 0.5
MOMENTUM = 0.9
RATE = 0.3
EPSILON = 1e-06
SIGNAL = 9.0


def passed_along(shard, axis, by):
    length = lax.axis_size(axis)
    return lax.ppermute(shard, axis, [(i, (i + by) % length) for i in range(length)])


def square_norms(row_block):
    widened = row_block.astype(jnp.float32)
    return jnp.sum(widened * widened, axis=-1)


def kernel_tile(left_rows, right_rows):
    dot_values = lax.dot_general(
        left_rows, right_rows, (((1,), (1,)), ((), ())), preferred_element_type=jnp.float32
    )
    distance = square_norms(left_rows)[:, None] + square_norms(right_rows)[None, :] - 2.0 * dot_values
    return SIGNAL * jnp.exp(-distance / left_rows.shape[1])


def product(left, right):
    return jnp.dot(left, right, precision=lax.Precision.HIGHEST)


def prior_values(cand_rows, frequencies, phases, prior_weight):
    angles = (
        jnp.dot(cand_rows, frequencies, preferred_element_type=jnp.float32) * math.sqrt(2.0)
        + phases[None, :]
    )
    features = math.sqrt(2.0 * SIGNAL / frequencies.shape[1]) * jnp.cos(angles)
    return product(features, prior_weight)


def geometric(first, last):
    return sum(MOMENTUM**i for i in range(first, last + 1))


def shards(
    records,
    coefficients,
    velocity,
    targets,
    block_local,
    block_count,
    candidates,
    frequencies,
    phases,
    prior_weight,
):
    n_blk = lax.axis_size("blk")
    record_total = records.shape[0] * n_blk
    root_count = jnp.sqrt(jnp.float32(record_total))
    steps, cap = block_local.shape
    own = lax.axis_index("blk")
    neighbour = passed_along(candidates, "blk", 1)
    picked = block_local.reshape(-1)
    gathered = lax.all_gather(records[picked], "blk", axis=0)
    ids = lax.all_gather(picked, "blk", axis=0) + (
        jnp.arange(n_blk, dtype=jnp.int32) * records.shape[0]
    )[:, None]
    rows, keys, partial = [], [], []
    for t in range(steps):
        part = slice(t * cap, (t + 1) * cap)
        rows.append(gathered[:, part].reshape(n_blk * cap, -1))
        keys.append(ids[:, part].reshape(-1))
        held = coefficients + geometric(1, t) * velocity
        local = product(kernel_tile(rows[t], records), held) / root_count
        mine = NOISE * held[block_local[t]] - targets[block_local[t]]
        before = lax.dynamic_slice_in_dim(local, own * cap, cap, 0)
        partial.append(lax.dynamic_update_slice_in_dim(local, before + mine, own * cap, 0))
    whole = lax.psum(jnp.stack(partial), "blk")
    moves = []
    for t in range(steps):
        gradient = whole[t]
        for s in range(t):
            link = kernel_tile(rows[t], rows[s]) / root_count + NOISE * (
                keys[t][:, None] == keys[s][None, :]
            ).astype(jnp.float32)
            gradient = gradient + geometric(0, t - 1 - s) * product(link, moves[s])
        live = (jnp.arange(cap, dtype=jnp.int32)[None, :] < block_count[t][:, None]).reshape(-1)
        moves.append(jnp.where(live[:, None], -RATE * gradient, 0.0))
    mine = [lax.dynamic_slice_in_dim(m, own * cap, cap, 0) for m in moves]
    speed = jnp.concatenate([MOMENTUM ** (steps - 1 - s) * m for s, m in enumerate(mine)])
    shift = jnp.concatenate([geometric(0, steps - 1 - s) * m for s, m in enumerate(mine)])
    both = jnp.concatenate(
        [
            coefficients + geometric(1, steps) * velocity,
            MOMENTUM**steps * velocity,
        ],
        axis=1,
    )
    both = both.at[picked].add(jnp.concatenate([shift, speed], axis=1))
    width = coefficients.shape[1]
    coefficients, velocity = both[:, :width], both[:, width:]
    own_sum = product(kernel_tile(candidates, records), coefficients)
    next_sum = product(kernel_tile(neighbour, records), coefficients)
    first_part = prior_values(candidates, frequencies, phases, prior_weight) + own_sum / root_count
    scores = passed_along(first_part, "blk", 2) + passed_along(next_sum / root_count, "blk", 1)
    squares_local = jnp.sum(scores * scores, axis=1)
    summed = lax.psum(squares_local, "path")
    path_rms = jnp.sqrt(summed / (scores.shape[1] * lax.axis_size("path")) + EPSILON)
    return (coefficients, velocity, scores, path_rms)


F32, BF16 = jnp.float32, jnp.bfloat16
TURN_PARTS = (6.28125, 0.001935482025146484, -1.748455600074e-07)
COS_TERMS = (1.0, -0.49999988079071045, 0.04166648909449577, -0.00138877984136343, 2.4769791707512923e-05, -2.707819533043221e-07, 1.7242244298998344e-09)
KEYS = 128
CHUNK = 256


def nt(left, right):
    return lax.dot_general(left, right, (((1,), (1,)), ((), ())), preferred_element_type=F32)


def nn(left, right):
    return lax.dot_general(left, right, (((1,), (0,)), ((), ())), preferred_element_type=F32)


def split(value, pieces):
    parts = []
    for _ in range(pieces):
        part = value.astype(BF16)
        parts.append(part)
        value = value - part.astype(F32)
    return parts


def stacked(value, pieces):
    return jnp.concatenate(split(value, pieces), axis=0)


def weighted(weights, tile, dot):
    rows = weights.shape[0]
    high, low = split(tile, 2)
    parts = stacked(weights, 2)
    both = dot(parts, high)
    return both[:rows] + both[rows:] + dot(parts[:rows], low)


def exactly(value, ones):
    rows = value.shape[0]
    thrice = nn(stacked(value, 3), ones)
    return thrice[:rows] + thrice[rows : 2 * rows] + thrice[2 * rows :]


def column_norms(rows):
    widened = rows.astype(F32)
    return jnp.sum(widened * widened, axis=1, keepdims=True)


def row_norms(rows):
    widened = rows.astype(F32)
    high, low = split(widened * widened, 2)
    ones = jnp.ones((16, rows.shape[1]), BF16)
    return (nt(ones, high) + nt(ones, low))[0:1]


def gaussian(left, left_norms, right, right_norms):
    return jnp.exp((2.0 * nt(left, right) - left_norms - right_norms) * (1.0 / left.shape[1]))


def cosine(angles):
    turns = jnp.round(angles * (1.0 / (2.0 * math.pi)))
    rest = angles
    for part in TURN_PARTS:
        rest = rest - turns * part
    square = rest * rest
    value = jnp.full_like(square, COS_TERMS[-1])
    for term in COS_TERMS[-2::-1]:
        value = value * square + term
    return value


def fused(
    n_blk, n_path,
    rec, coef, vel, targ, local, count, cand, freq, phase, weight,
    coef_out, vel_out, score_out, rms_out,
    xs, cand_in, partial, first_buf, second_buf, first_in, second_in, squares, local_pad,
    link_high, link_low, kx,
    x_send, x_recv, c_send, c_recv, p_send, p_recv, s_send, s_recv, q_send, q_recv,
):
    steps, cap = local.shape
    recs, width = rec.shape
    group = cand.shape[0]
    paths = coef.shape[0]
    slots = xs.shape[0] // n_blk
    total = xs.shape[0]
    root = math.sqrt(recs * n_blk)
    scale = SIGNAL / root
    me, my_path = lax.axis_index("blk"), lax.axis_index("path")

    def peer(by):
        return lax.rem(me + by, n_blk)

    def beside(by):
        return lax.rem(my_path + by, n_path)

    barrier = pltpu.get_barrier_semaphore()
    for by in range(1, n_blk):
        pl.semaphore_signal(barrier, inc=1, device_id={"blk": peer(by)}, device_id_type=pl.DeviceIdType.MESH)
    for by in range(1, n_path):
        pl.semaphore_signal(barrier, inc=1, device_id={"path": beside(by)}, device_id_type=pl.DeviceIdType.MESH)

    def remote(src, dst, send, recv, target):
        return pltpu.make_async_remote_copy(
            src_ref=src, dst_ref=dst, send_sem=send, recv_sem=recv,
            device_id=target, device_id_type=pl.DeviceIdType.MESH,
        )

    local_pad[...] = jnp.zeros_like(local_pad)
    local_pad[0:steps, 0:cap] = local[...].astype(F32)
    turned = jnp.transpose(local_pad[...])
    picked = jnp.concatenate(
        [turned[0:cap, t : t + 1] for t in range(steps)]
        + [jnp.full((slots - steps * cap, 1), -1.0, F32)],
        axis=0,
    )
    lanes = lax.broadcasted_iota(jnp.int32, (slots, recs), 1).astype(F32)
    chosen = (picked == lanes).astype(BF16)
    high_digit = jnp.floor(picked * (1.0 / 32.0))
    low_digit = picked - 32.0 * high_digit
    lane = lax.broadcasted_iota(jnp.int32, (slots, KEYS), 1)
    digits = jnp.where(lane == 0, high_digit, jnp.where(lane == 1, low_digit, 0.0))
    mine = nn(chosen, rec[...]).astype(BF16)
    block = pl.ds(pl.multiple_of(me * slots, slots), slots)
    xs[block, 0:width] = mine
    xs[block, width : width + KEYS] = digits.astype(BF16)

    pl.semaphore_wait(barrier, n_blk - 1 + n_path - 1)
    sends = []
    for by in range(1, n_blk):
        copy = remote(xs.at[block], xs.at[block], x_send.at[by], x_recv.at[by], {"blk": peer(by)})
        copy.start()
        sends.append(copy)
    cand_copy = remote(cand, cand_in, c_send, c_recv, {"blk": peer(1)})
    cand_copy.start()
    sends.append(cand_copy)

    start, speed0 = coef[...], vel[...]
    base = (start + geometric(1, steps) * speed0) * scale
    rec_norms = column_norms(rec[...])
    mine_norms = column_norms(mine)

    def base_values(rows):
        norms = row_norms(rows)
        value = jnp.zeros((paths, group), F32)
        for c in range(0, recs, CHUNK):
            tile = gaussian(rec[c : c + CHUNK, :], rec_norms[c : c + CHUNK], rows, norms)
            value = value + weighted(base[:, c : c + CHUNK], tile, nn)
        return value, gaussian(mine, mine_norms, rows, norms)

    feats = freq.shape[1]
    amplitude = weight[...] * math.sqrt(2.0 * SIGNAL / feats)
    first = jnp.zeros((paths, group), F32)
    for c in range(0, feats, CHUNK):
        part = slice(c, c + CHUNK)
        angles = nn(cand[...], freq[:, part]) * math.sqrt(2.0) + phase[:, part]
        first = first + weighted(amplitude[:, part], cosine(angles), nt)
    value, near = base_values(cand[...])
    first_buf[...] = first + value
    kx[:, 0:group] = near

    for by in range(1, n_blk):
        source = pl.ds(pl.multiple_of(peer(n_blk - by) * slots, slots), slots)
        remote(xs.at[source], xs.at[source], x_send.at[by], x_recv.at[by], {"blk": peer(by)}).wait_recv()
    points = xs[:, 0:width]
    point_digits = xs[:, width : width + KEYS]
    digit_lane = lax.broadcasted_iota(jnp.int32, (16, KEYS), 1)
    digit_worth = jnp.where(digit_lane == 0, 32.0, jnp.where(digit_lane == 1, 1.0, 0.0)).astype(BF16)
    place_row = lax.broadcasted_iota(jnp.int32, (1, total), 1).astype(F32)
    place_col = lax.broadcasted_iota(jnp.int32, (total, 1), 0).astype(F32)
    owner_row = jnp.floor((place_row + 0.5) * (1.0 / slots))
    owner_col = jnp.floor((place_col + 0.5) * (1.0 / slots))
    step_row = jnp.floor((place_row - slots * owner_row + 0.5) * (1.0 / cap))
    step_col = jnp.floor((place_col - slots * owner_col + 0.5) * (1.0 / cap))
    key_row = nt(digit_worth, point_digits)[0:1] + recs * owner_row
    spread = point_digits.astype(F32)
    key_col = 32.0 * spread[:, 0:1] + spread[:, 1:2] + recs * owner_col
    point_norms = row_norms(points)

    def by_step(step, values):
        out = jnp.zeros_like(step)
        for t, entry in enumerate(values):
            out = jnp.where(step == t, entry, out)
        return out

    me_first = (me * recs).astype(F32)
    held = jnp.concatenate([start, speed0], axis=0)
    sums = jnp.zeros((2 * paths, total), F32)
    owed = jnp.zeros((paths, total), F32)
    for c in range(0, recs, CHUNK):
        part = slice(c, c + CHUNK)
        ids = lax.broadcasted_iota(jnp.int32, (CHUNK, 1), 0).astype(F32) + (me_first + c)
        here = (ids == key_row).astype(F32)
        tile = gaussian(rec[part, :], rec_norms[part], points, point_norms) * scale + NOISE * here
        sums = sums + weighted(held[:, part], tile, nn)
        owed = owed + exactly(targ[:, part], here.astype(BF16))
    ahead = by_step(step_row, [geometric(1, t) for t in range(steps)])
    partial[me] = sums[:paths] + ahead * sums[paths:] - owed
    for by in range(1, n_blk):
        copy = remote(partial.at[me], partial.at[me], p_send.at[by], p_recv.at[by], {"blk": peer(by)})
        copy.start()
        sends.append(copy)

    for c in range(0, total, 128):
        part = slice(c, c + 128)
        same = (key_col[part] == key_row).astype(F32)
        tile = gaussian(points[part], column_norms(points[part]), points, point_norms) * scale + NOISE * same
        factor = by_step(
            step_row - step_col[part] - 1.0, [geometric(0, d) for d in range(steps - 1)]
        )
        factor = jnp.where(step_row < steps, factor, 0.0)
        high, low = split(tile * factor, 2)
        link_high[part, :] = high
        link_low[part, :] = low
    cand_copy.wait_recv()
    value, near = base_values(cand_in[...])
    second_buf[...] = value
    kx[:, group : 2 * group] = near
    live = jnp.zeros((1, total), F32)
    for t in range(steps):
        for o in range(n_blk):
            begin = float(o * slots + t * cap)
            upto = begin + count[t, o].astype(F32)
            live = jnp.where((place_row >= begin) & (place_row < upto), -RATE, live)
    select = (
        lax.broadcasted_iota(jnp.int32, (total, slots), 0)
        == lax.broadcasted_iota(jnp.int32, (total, slots), 1) + me * slots
    ).astype(BF16)

    for by in range(1, n_blk):
        source = peer(n_blk - by)
        remote(partial.at[source], partial.at[source], p_send.at[by], p_recv.at[by], {"blk": peer(by)}).wait_recv()
    gradient = partial[0]
    for o in range(1, n_blk):
        gradient = gradient + partial[o]
    moves = gradient * live
    for _ in range(steps - 1):
        parts = stacked(moves, 2)
        both = nn(parts, link_high[...])
        acted = both[:paths] + both[paths:] + nn(parts[:paths], link_low[...])
        moves = (gradient + acted) * live
    shift = moves * by_step(step_row, [geometric(0, steps - 1 - t) for t in range(steps)])
    kick = moves * by_step(step_row, [MOMENTUM ** (steps - 1 - t) for t in range(steps)])
    ours = exactly(jnp.concatenate([shift, kick], axis=0), select)

    late = weighted(ours[:paths] * scale, kx[...], nn)
    first_buf[...] = first_buf[...] + late[:, 0:group]
    second_buf[...] = second_buf[...] + late[:, group : 2 * group]
    first_copy = remote(first_buf, first_in, s_send.at[0], s_recv.at[0], {"blk": peer(2)})
    second_copy = remote(second_buf, second_in, s_send.at[1], s_recv.at[1], {"blk": peer(1)})
    first_copy.start()
    second_copy.start()
    sends += [first_copy, second_copy]
    added = exactly(ours, chosen)
    coef_out[...] = start + geometric(1, steps) * speed0 + added[:paths]
    vel_out[...] = MOMENTUM**steps * speed0 + added[paths:]
    first_copy.wait_recv()
    second_copy.wait_recv()
    scores = first_in[...] + second_in[...]
    score_out[...] = scores
    squares[my_path] = jnp.broadcast_to(jnp.sum(scores * scores, axis=0, keepdims=True), (8, group))
    for by in range(1, n_path):
        copy = remote(squares.at[my_path], squares.at[my_path], q_send.at[by], q_recv.at[by], {"path": beside(by)})
        copy.start()
        sends.append(copy)
    for by in range(1, n_path):
        source = beside(n_path - by)
        remote(squares.at[source], squares.at[source], q_send.at[by], q_recv.at[by], {"path": beside(by)}).wait_recv()
    summed = squares[0]
    for z in range(1, n_path):
        summed = summed + squares[z]
    rms_out[...] = jnp.sqrt(summed * (1.0 / (paths * n_path)) + EPSILON)[0:1]
    for copy in sends:
        copy.wait_send()


def fused_shards(
    n_blk, n_path,
    records, coefficients, velocity, targets, block_local, block_count,
    candidates, frequencies, phases, prior_weight,
):
    steps, cap = block_local.shape
    recs, width = records.shape
    group, paths = candidates.shape[0], coefficients.shape[1]
    slots = -(-(steps * cap + 1) // 16) * 16
    total = n_blk * slots
    vmem = pl.BlockSpec(memory_space=pltpu.VMEM)
    outs = pl.pallas_call(
        functools.partial(fused, n_blk, n_path),
        out_shape=(
            jax.ShapeDtypeStruct((paths, recs), F32),
            jax.ShapeDtypeStruct((paths, recs), F32),
            jax.ShapeDtypeStruct((paths, group), F32),
            jax.ShapeDtypeStruct((1, group), F32),
        ),
        in_specs=[vmem] * 5 + [pl.BlockSpec(memory_space=pltpu.SMEM)] + [vmem] * 4,
        out_specs=(vmem,) * 4,
        scratch_shapes=[
            pltpu.VMEM((total, width + KEYS), BF16),
            pltpu.VMEM((group, width), BF16),
            pltpu.VMEM((n_blk, paths, total), F32),
            pltpu.VMEM((paths, group), F32),
            pltpu.VMEM((paths, group), F32),
            pltpu.VMEM((paths, group), F32),
            pltpu.VMEM((paths, group), F32),
            pltpu.VMEM((n_path, 8, group), F32),
            pltpu.VMEM((8, 128), F32),
            pltpu.VMEM((total, total), BF16),
            pltpu.VMEM((total, total), BF16),
            pltpu.VMEM((slots, 2 * group), F32),
            pltpu.SemaphoreType.DMA((n_blk,)),
            pltpu.SemaphoreType.DMA((n_blk,)),
            pltpu.SemaphoreType.DMA,
            pltpu.SemaphoreType.DMA,
            pltpu.SemaphoreType.DMA((n_blk,)),
            pltpu.SemaphoreType.DMA((n_blk,)),
            pltpu.SemaphoreType.DMA((2,)),
            pltpu.SemaphoreType.DMA((2,)),
            pltpu.SemaphoreType.DMA((n_path,)),
            pltpu.SemaphoreType.DMA((n_path,)),
        ],
        compiler_params=pltpu.CompilerParams(
            collective_id=0, has_side_effects=True, vmem_limit_bytes=48 * 1024 * 1024
        ),
    )(
        records, coefficients.T, velocity.T, targets.T, block_local, block_count,
        candidates, frequencies, phases.reshape(1, -1), prior_weight.T,
    )
    return (outs[0].T, outs[1].T, outs[2].T, outs[3].reshape(-1))


def solution(mesh):

    n_blk, n_path = mesh.shape["blk"], mesh.shape["path"]
    body = functools.partial(fused_shards, n_blk, n_path) if n_blk <= 16 else shards
    return jax.shard_map(
        body,
        mesh=mesh,
        in_specs=(
            P("blk", None),
            P("blk", "path"),
            P("blk", "path"),
            P("blk", "path"),
            P(None, "blk"),
            P(),
            P("blk", None),
            P(),
            P(),
            P(None, "path"),
        ),
        out_specs=(P("blk", "path"), P("blk", "path"), P("blk", "path"), P("blk")),
        check_vma=False,
    )
```

profile of v0, /device:TPU:0, one launch (start us, length us, event | category | flops | bytes accessed | tf_op | source)
XLA Modules:
  0.0 45.5 jit_solution(276875912703873704)
XLA Ops:
  0.6 0.0 copy-start.9
  0.6 0.0 copy-start.7
  0.7 0.0 copy-start.8
  0.7 0.7 %copy-done.9 = s32[3,8]{1,0:T(4,128)S(1)} copy-done((s32[3,8]{1,0:T(4,128)S(1)}, s32[3,8]{1,0:T(4,128)}, u32[]{:S(2)}) %copy-start.9) | copy-done | bytes 120
  1.3 0.0 copy-done.7
  1.3 0.0 copy-done.8
  1.3 0.0 copy-start
  1.4 1.2 %copy-done = bf16[1024,512]{1,0:T(8,128)(2,1)S(1)} copy-done((bf16[1024,512]{1,0:T(8,128)(2,1)S(1)}, bf16[1024,512]{1,0:T(8,128)(2,1)}, u32[]{:S(2)}) %copy-start) | copy-done | bytes 1048600
  2.6 0.0 copy-start.1
  2.6 1.2 %copy-done.1 = bf16[512,1024]{1,0:T(8,128)(2,1)S(1)} copy-done((bf16[512,1024]{1,0:T(8,128)(2,1)S(1)}, bf16[512,1024]{1,0:T(8,128)(2,1)}, u32[]{:S(2)}) %copy-start.1) | copy-done | bytes 1048600
  3.8 0.0 copy-start.2
  3.8 1.0 %copy-done.2 = bf16[512,512]{1,0:T(8,128)(2,1)S(1)} copy-done((bf16[512,512]{1,0:T(8,128)(2,1)S(1)}, bf16[512,512]{1,0:T(8,128)(2,1)}, u32[]{:S(2)}) %copy-start.2) | copy-done | bytes 524312
  4.8 0.0 copy-start.3
  4.8 0.8 %copy-done.3 = f32[1024,16]{0,1:T(8,128)S(1)} copy-done((f32[1024,16]{0,1:T(8,128)S(1)}, f32[1024,16]{0,1:T(8,128)}, u32[]{:S(2)}) %copy-start.3) | copy-done | bytes 65560
  5.7 0.0 copy-start.4
  5.7 0.8 %copy-done.4 = f32[1024,16]{0,1:T(8,128)S(1)} copy-done((f32[1024,16]{0,1:T(8,128)S(1)}, f32[1024,16]{0,1:T(8,128)}, u32[]{:S(2)}) %copy-start.4) | copy-done | bytes 65560
  6.5 0.0 copy-start.5
  6.5 0.8 %copy-done.5 = f32[1024,16]{0,1:T(8,128)S(1)} copy-done((f32[1024,16]{0,1:T(8,128)S(1)}, f32[1024,16]{0,1:T(8,128)}, u32[]{:S(2)}) %copy-start.5) | copy-done | bytes 65560
  7.4 0.0 copy-start.6
  7.4 0.8 %copy-done.6 = f32[1024,16]{0,1:T(8,128)S(1)} copy-done((f32[1024,16]{0,1:T(8,128)S(1)}, f32[1024,16]{0,1:T(8,128)}, u32[]{:S(2)}) %copy-start.6) | copy-done | bytes 65560
  8.2 34.8 %shard_map.129 = (f32[16,1024]{1,0:T(8,128)S(1)}, f32[16,1024]{1,0:T(8,128)S(1)}, f32[16,512]{1,0:T(8,128)S(1)}, f32[1,512]{1,0:T(1,128)S(1)}) custom-call(bf16[1024,512]{1,0:T(8,128)(2,1)S(1)} %copy-done, f32[16,1024]{1,0:T(8,128)S(1)} %bitcast.9, f32[16,1024]{1,0:T(8,128)S(1)} %bitcast.10, f32[16,1024]{1,0:T(8,128)S(1)} %bitcast.11, ...), custom_call_target="tpu_custom_call" | custom-call | tf_op jit(solution)/shard_map/pallas_call | solution.py:405
  43.0 0.6 %copy.18 = f32[1024,16]{0,1:T(8,128)} copy(f32[1024,16]{0,1:T(8,128)S(1)} %bitcast.14) | data formatting | bytes 131072
  43.7 0.6 %copy.19 = f32[1024,16]{0,1:T(8,128)} copy(f32[1024,16]{0,1:T(8,128)S(1)} %bitcast.13) | data formatting | bytes 131072
  44.3 0.6 %copy.20 = f32[512,16]{0,1:T(8,128)} copy(f32[512,16]{0,1:T(8,128)S(1)} %bitcast.15) | data formatting | bytes 65536
  44.9 0.6 %copy.21 = f32[512]{0:T(512)} copy(f32[512]{0:T(512)S(1)} %bitcast.17) | data formatting | bytes 4096
Async XLA Ops:
  0.6 0.7 %copy-start.9 = (s32[3,8]{1,0:T(4,128)S(1)}, s32[3,8]{1,0:T(4,128)}, u32[]{:S(2)}) copy-start(s32[3,8]{1,0:T(4,128)} %count.1) | copy-start | bytes 292
  0.6 0.7 %copy-start.7 = (f32[1024]{0:T(1024)S(1)}, f32[1024]{0:T(1024)}, u32[]{:S(2)}) copy-start(f32[1024]{0:T(1024)} %param.18) | copy-start | bytes 12292
  0.7 0.7 %copy-start.8 = (s32[3,24]{1,0:T(4,128)S(1)}, s32[3,24]{1,0:T(4,128)}, u32[]{:S(2)}) copy-start(s32[3,24]{1,0:T(4,128)} %local.1) | copy-start | bytes 868
  1.3 1.2 %copy-start = (bf16[1024,512]{1,0:T(8,128)(2,1)S(1)}, bf16[1024,512]{1,0:T(8,128)(2,1)}, u32[]{:S(2)}) copy-start(bf16[1024,512]{1,0:T(8,128)(2,1)} %rec.1) | copy-start | bytes 3145732
  2.6 1.2 %copy-start.1 = (bf16[512,1024]{1,0:T(8,128)(2,1)S(1)}, bf16[512,1024]{1,0:T(8,128)(2,1)}, u32[]{:S(2)}) copy-start(bf16[512,1024]{1,0:T(8,128)(2,1)} %freq.1) | copy-start | bytes 3145732
  3.8 1.0 %copy-start.2 = (bf16[512,512]{1,0:T(8,128)(2,1)S(1)}, bf16[512,512]{1,0:T(8,128)(2,1)}, u32[]{:S(2)}) copy-start(bf16[512,512]{1,0:T(8,128)(2,1)} %cand.1) | copy-start | bytes 1572868
  4.8 0.8 %copy-start.3 = (f32[1024,16]{0,1:T(8,128)S(1)}, f32[1024,16]{0,1:T(8,128)}, u32[]{:S(2)}) copy-start(f32[1024,16]{0,1:T(8,128)} %param.11) | copy-start | bytes 196612
  5.7 0.8 %copy-start.4 = (f32[1024,16]{0,1:T(8,128)S(1)}, f32[1024,16]{0,1:T(8,128)}, u32[]{:S(2)}) copy-start(f32[1024,16]{0,1:T(8,128)} %param.12) | copy-start | bytes 196612
  6.5 0.8 %copy-start.5 = (f32[1024,16]{0,1:T(8,128)S(1)}, f32[1024,16]{0,1:T(8,128)}, u32[]{:S(2)}) copy-start(f32[1024,16]{0,1:T(8,128)} %param.13) | copy-start | bytes 196612
  7.4 0.8 %copy-start.6 = (f32[1024,16]{0,1:T(8,128)S(1)}, f32[1024,16]{0,1:T(8,128)}, u32[]{:S(2)}) copy-start(f32[1024,16]{0,1:T(8,128)} %param.19) | copy-start | bytes 196612
where the time goes:
time: 46 us; the launch traced here: 45.5 us
  Pallas kernels  34.8 us (76%)
  local copies, waits for them, and re-layouts  9.99 us (22%)
  between operations  0.68 us (1%)
    pallas_call x1, Pallas kernels, fused_shards(): pl.pallas_call(functools.partial(fused, n_blk, n_path), out_shape=(jax.Sh...  34.8 us
    unnamed x24, local copies, waits for them, and re-layouts  9.99 us

commit v1 on v0

--- a/solution.py
+++ b/solution.py
@@ -164,15 +164,22 @@
     return jnp.sum(widened * widened, axis=1, keepdims=True)
 
 
+def as_lanes(columns):
+    rows = columns[0].shape[0]
+    lane = lax.broadcasted_iota(jnp.int32, (rows, KEYS), 1)
+    out = jnp.zeros((rows, KEYS), F32)
+    for at, column in enumerate(columns):
+        out = jnp.where(lane == at, column.astype(F32), out)
+    return out.astype(BF16)
+
+
 def row_norms(rows):
-    widened = rows.astype(F32)
-    high, low = split(widened * widened, 2)
-    ones = jnp.ones((16, rows.shape[1]), BF16)
-    return (nt(ones, high) + nt(ones, low))[0:1]
+    return nt(jnp.ones((16, KEYS), BF16), as_lanes(split(column_norms(rows), 3)))[0:1]
 
 
 def gaussian(left, left_norms, right, right_norms):
-    return jnp.exp((2.0 * nt(left, right) - left_norms - right_norms) * (1.0 / left.shape[1]))
+    rate = math.log2(math.e) / left.shape[1]
+    return jnp.exp2(nt(left, right) * (2.0 * rate) - left_norms * rate - right_norms * rate)
 
 
 def cosine(angles):
@@ -189,10 +196,11 @@
 
 def fused(
     n_blk, n_path,
-    rec, coef, vel, targ, local, count, cand, freq, phase, weight,
+    rec_hbm, coef_hbm, vel_hbm, targ_hbm, local_hbm, count_hbm, cand_hbm, freq_hbm, phase_hbm, weight_hbm,
     coef_out, vel_out, score_out, rms_out,
     xs, cand_in, partial, first_buf, second_buf, first_in, second_in, squares, local_pad,
     link_high, link_low, kx,
+    rec, coef, vel, targ, local, count, cand, freq, phase, weight, loaded,
     x_send, x_recv, c_send, c_recv, p_send, p_recv, s_send, s_recv, q_send, q_recv,
 ):
     steps, cap = local.shape
@@ -203,6 +211,13 @@
     total = xs.shape[0]
     root = math.sqrt(recs * n_blk)
     scale = SIGNAL / root
+    fetched = [
+        (local_hbm, local), (rec_hbm, rec), (cand_hbm, cand), (coef_hbm, coef), (vel_hbm, vel),
+        (targ_hbm, targ), (weight_hbm, weight), (phase_hbm, phase), (freq_hbm, freq), (count_hbm, count),
+    ]
+    fetches = [pltpu.make_async_copy(a, b, loaded.at[i]) for i, (a, b) in enumerate(fetched)]
+    for fetch in fetches:
+        fetch.start()
     me, my_path = lax.axis_index("blk"), lax.axis_index("path")
 
     def peer(by):
@@ -224,6 +239,7 @@
         )
 
     local_pad[...] = jnp.zeros_like(local_pad)
+    fetches[0].wait()
     local_pad[0:steps, 0:cap] = local[...].astype(F32)
     turned = jnp.transpose(local_pad[...])
     picked = jnp.concatenate(
@@ -235,12 +251,12 @@
     chosen = (picked == lanes).astype(BF16)
     high_digit = jnp.floor(picked * (1.0 / 32.0))
     low_digit = picked - 32.0 * high_digit
-    lane = lax.broadcasted_iota(jnp.int32, (slots, KEYS), 1)
-    digits = jnp.where(lane == 0, high_digit, jnp.where(lane == 1, low_digit, 0.0))
+    fetches[1].wait()
     mine = nn(chosen, rec[...]).astype(BF16)
+    mine_norms = column_norms(mine)
     block = pl.ds(pl.multiple_of(me * slots, slots), slots)
     xs[block, 0:width] = mine
-    xs[block, width : width + KEYS] = digits.astype(BF16)
+    xs[block, width : width + KEYS] = as_lanes([high_digit, low_digit] + split(mine_norms, 3))
 
     pl.semaphore_wait(barrier, n_blk - 1 + n_path - 1)
     sends = []
@@ -248,14 +264,23 @@
         copy = remote(xs.at[block], xs.at[block], x_send.at[by], x_recv.at[by], {"blk": peer(by)})
         copy.start()
         sends.append(copy)
+    fetches[2].wait()
     cand_copy = remote(cand, cand_in, c_send, c_recv, {"blk": peer(1)})
     cand_copy.start()
     sends.append(cand_copy)
 
+    for fetch in fetches[3:]:
+        fetch.wait()
     start, speed0 = coef[...], vel[...]
+    at_mine = jnp.concatenate([start, speed0, targ[...]], axis=0)
+    thrice = nt(stacked(at_mine, 3), chosen)
+    at_mine = thrice[: 3 * paths] + thrice[3 * paths : 6 * paths] + thrice[6 * paths :]
+    select = (
+        lax.broadcasted_iota(jnp.int32, (total, slots), 0)
+        == lax.broadcasted_iota(jnp.int32, (total, slots), 1) + me * slots
+    ).astype(BF16)
     base = (start + geometric(1, steps) * speed0) * scale
     rec_norms = column_norms(rec[...])
-    mine_norms = column_norms(mine)
 
     def base_values(rows):
         norms = row_norms(rows)
@@ -282,17 +307,21 @@
     points = xs[:, 0:width]
     point_digits = xs[:, width : width + KEYS]
     digit_lane = lax.broadcasted_iota(jnp.int32, (16, KEYS), 1)
-    digit_worth = jnp.where(digit_lane == 0, 32.0, jnp.where(digit_lane == 1, 1.0, 0.0)).astype(BF16)
+    digit_line = lax.broadcasted_iota(jnp.int32, (16, KEYS), 0)
+    digit_worth = jnp.where(digit_lane == 0, 32.0, jnp.where(digit_lane == 1, 1.0, 0.0))
+    norm_worth = jnp.where((digit_lane >= 2) & (digit_lane < 5), 1.0, 0.0)
+    worth = jnp.where(digit_line == 0, digit_worth, norm_worth).astype(BF16)
     place_row = lax.broadcasted_iota(jnp.int32, (1, total), 1).astype(F32)
     place_col = lax.broadcasted_iota(jnp.int32, (total, 1), 0).astype(F32)
     owner_row = jnp.floor((place_row + 0.5) * (1.0 / slots))
     owner_col = jnp.floor((place_col + 0.5) * (1.0 / slots))
     step_row = jnp.floor((place_row - slots * owner_row + 0.5) * (1.0 / cap))
     step_col = jnp.floor((place_col - slots * owner_col + 0.5) * (1.0 / cap))
-    key_row = nt(digit_worth, point_digits)[0:1] + recs * owner_row
+    read = nt(worth, point_digits)
+    key_row, point_norms = read[0:1] + recs * owner_row, read[1:2]
     spread = point_digits.astype(F32)
     key_col = 32.0 * spread[:, 0:1] + spread[:, 1:2] + recs * owner_col
-    point_norms = row_norms(points)
+    norms_col = spread[:, 2:3] + spread[:, 3:4] + spread[:, 4:5]
 
     def by_step(step, values):
         out = jnp.zeros_like(step)
@@ -300,17 +329,16 @@
             out = jnp.where(step == t, entry, out)
         return out
 
-    me_first = (me * recs).astype(F32)
-    held = jnp.concatenate([start, speed0], axis=0)
+    held = jnp.concatenate([start, speed0], axis=0) * scale
     sums = jnp.zeros((2 * paths, total), F32)
-    owed = jnp.zeros((paths, total), F32)
     for c in range(0, recs, CHUNK):
         part = slice(c, c + CHUNK)
-        ids = lax.broadcasted_iota(jnp.int32, (CHUNK, 1), 0).astype(F32) + (me_first + c)
-        here = (ids == key_row).astype(F32)
-        tile = gaussian(rec[part, :], rec_norms[part], points, point_norms) * scale + NOISE * here
+        tile = gaussian(rec[part, :], rec_norms[part], points, point_norms)
         sums = sums + weighted(held[:, part], tile, nn)
-        owed = owed + exactly(targ[:, part], here.astype(BF16))
+    placed = nt(stacked(at_mine, 3), select)
+    placed = placed[: 3 * paths] + placed[3 * paths : 6 * paths] + placed[6 * paths :]
+    sums = sums + NOISE * placed[: 2 * paths]
+    owed = placed[2 * paths :]
     ahead = by_step(step_row, [geometric(1, t) for t in range(steps)])
     partial[me] = sums[:paths] + ahead * sums[paths:] - owed
     for by in range(1, n_blk):
@@ -321,7 +349,7 @@
     for c in range(0, total, 128):
         part = slice(c, c + 128)
         same = (key_col[part] == key_row).astype(F32)
-        tile = gaussian(points[part], column_norms(points[part]), points, point_norms) * scale + NOISE * same
+        tile = gaussian(points[part], norms_col[part], points, point_norms) * scale + NOISE * same
         factor = by_step(
             step_row - step_col[part] - 1.0, [geometric(0, d) for d in range(steps - 1)]
         )
@@ -339,11 +367,6 @@
             begin = float(o * slots + t * cap)
             upto = begin + count[t, o].astype(F32)
             live = jnp.where((place_row >= begin) & (place_row < upto), -RATE, live)
-    select = (
-        lax.broadcasted_iota(jnp.int32, (total, slots), 0)
-        == lax.broadcasted_iota(jnp.int32, (total, slots), 1) + me * slots
-    ).astype(BF16)
-
     for by in range(1, n_blk):
         source = peer(n_blk - by)
         remote(partial.at[source], partial.at[source], p_send.at[by], p_recv.at[by], {"blk": peer(by)}).wait_recv()
@@ -391,6 +414,15 @@
         copy.wait_send()
 
 
+def written(a, b, c, d, to_a, to_b, to_c, to_d, done):
+    pairs = [(a, to_a), (b, to_b), (c, to_c), (d, to_d)]
+    copies = [pltpu.make_async_copy(x, y, done.at[i]) for i, (x, y) in enumerate(pairs)]
+    for copy in copies:
+        copy.start()
+    for copy in copies:
+        copy.wait()
+
+
 def fused_shards(
     n_blk, n_path,
     records, coefficients, velocity, targets, block_local, block_count,
@@ -401,7 +433,7 @@
     group, paths = candidates.shape[0], coefficients.shape[1]
     slots = -(-(steps * cap + 1) // 16) * 16
     total = n_blk * slots
-    vmem = pl.BlockSpec(memory_space=pltpu.VMEM)
+    vmem, hbm = pl.BlockSpec(memory_space=pltpu.VMEM), pl.BlockSpec(memory_space=pltpu.HBM)
     outs = pl.pallas_call(
         functools.partial(fused, n_blk, n_path),
         out_shape=(
@@ -410,7 +442,7 @@
             jax.ShapeDtypeStruct((paths, group), F32),
             jax.ShapeDtypeStruct((1, group), F32),
         ),
-        in_specs=[vmem] * 5 + [pl.BlockSpec(memory_space=pltpu.SMEM)] + [vmem] * 4,
+        in_specs=[hbm] * 10,
         out_specs=(vmem,) * 4,
         scratch_shapes=[
             pltpu.VMEM((total, width + KEYS), BF16),
@@ -425,6 +457,17 @@
             pltpu.VMEM((total, total), BF16),
             pltpu.VMEM((total, total), BF16),
             pltpu.VMEM((slots, 2 * group), F32),
+            pltpu.VMEM(records.shape, BF16),
+            pltpu.VMEM((paths, recs), F32),
+            pltpu.VMEM((paths, recs), F32),
+            pltpu.VMEM((paths, recs), F32),
+            pltpu.VMEM(block_local.shape, jnp.int32),
+            pltpu.SMEM(block_count.shape, jnp.int32),
+            pltpu.VMEM(candidates.shape, BF16),
+            pltpu.VMEM(frequencies.shape, BF16),
+            pltpu.VMEM((1, phases.shape[0]), F32),
+            pltpu.VMEM((paths, phases.shape[0]), F32),
+            pltpu.SemaphoreType.DMA((10,)),
             pltpu.SemaphoreType.DMA((n_blk,)),
             pltpu.SemaphoreType.DMA((n_blk,)),
             pltpu.SemaphoreType.DMA,
@@ -437,12 +480,20 @@
             pltpu.SemaphoreType.DMA((n_path,)),
         ],
         compiler_params=pltpu.CompilerParams(
-            collective_id=0, has_side_effects=True, vmem_limit_bytes=48 * 1024 * 1024
+            collective_id=0, has_side_effects=True, vmem_limit_bytes=60 * 1024 * 1024
         ),
     )(
         records, coefficients.T, velocity.T, targets.T, block_local, block_count,
         candidates, frequencies, phases.reshape(1, -1), prior_weight.T,
     )
+    outs = pl.pallas_call(
+        written,
+        out_shape=[jax.ShapeDtypeStruct(o.shape, o.dtype) for o in outs],
+        in_specs=[hbm] * 4,
+        out_specs=[hbm] * 4,
+        scratch_shapes=[pltpu.SemaphoreType.DMA((4,))],
+        compiler_params=pltpu.CompilerParams(vmem_limit_bytes=60 * 1024 * 1024),
+    )(*outs)
     return (outs[0].T, outs[1].T, outs[2].T, outs[3].reshape(-1))
 
 

time: 46 us -> 42 us (0.913)
  local copies, waits for them, and re-layouts: 9.99 us -> 0 us
  Pallas kernels: 34.8 us -> 41.2 us
    unnamed x24 -> x0, local copies, waits for them, and re-layouts: 9.99 us -> none
    pallas_call x0 -> x1, Pallas kernels: none -> 6.16 us  [fused_shards(): pl.pallas_call(written, out_shape=[jax.ShapeDtypeStruct(o.shape, o.dtype)...]
where the time goes in v1:
time: 42 us; the launch traced here: 41.8 us
  Pallas kernels  41.2 us (98%)
  between operations  0.64 us (2%)
    pallas_call x1, Pallas kernels, fused_shards(): pl.pallas_call(functools.partial(fused, n_blk, n_path), out_shape=(jax.Sh...  35 us
    pallas_call x1, Pallas kernels, fused_shards(): pl.pallas_call(written, out_shape=[jax.ShapeDtypeStruct(o.shape, o.dtype)...  6.16 us

profile of v1, /device:TPU:0, one launch (start us, length us, event | category | flops | bytes accessed | tf_op | source)
XLA Modules:
  0.0 41.8 jit_solution(12790448514490284808)
XLA Ops:
  0.6 35.0 %shard_map.129 = (f32[16,1024]{1,0:T(8,128)}, f32[16,1024]{1,0:T(8,128)}, f32[16,512]{1,0:T(8,128)}, f32[1,512]{1,0:T(1,128)}) custom-call(bf16[1024,512]{1,0:T(8,128)(2,1)} %rec_hbm.1, f32[16,1024]{1,0:T(8,128)} %bitcast.9, f32[16,1024]{1,0:T(8,128)} %bitcast.10, f32[16,1024]{1,0:T(8,128)} %bitcast.11, s32[3,24]{1,0:T(4,128)} %local_hbm.1, ...), custom_call_target="tpu_custom_call" | custom-call | tf_op jit(solution)/shard_map/pallas_call | solution.py:437
  35.7 6.2 %shard_map.130 = (f32[16,1024]{1,0:T(8,128)}, f32[16,1024]{1,0:T(8,128)}, f32[16,512]{1,0:T(8,128)}, f32[1,512]{1,0:T(1,128)}) custom-call(f32[16,1024]{1,0:T(8,128)} %get-tuple-element.12.a, f32[16,1024]{1,0:T(8,128)} %get-tuple-element.13.b, f32[16,512]{1,0:T(8,128)} %get-tuple-element.14.c, f32[1,512]{1,0:T(1,128)} %get-tuple-element.15.d), custom_call_target="tpu_custom_call" | custom-call | tf_op jit(solution)/shard_map/pallas_call | solution.py:489

commit v2 on v1

--- a/solution.py
+++ b/solution.py
@@ -414,13 +414,8 @@
         copy.wait_send()
 
 
-def written(a, b, c, d, to_a, to_b, to_c, to_d, done):
-    pairs = [(a, to_a), (b, to_b), (c, to_c), (d, to_d)]
-    copies = [pltpu.make_async_copy(x, y, done.at[i]) for i, (x, y) in enumerate(pairs)]
-    for copy in copies:
-        copy.start()
-    for copy in copies:
-        copy.wait()
+def written(a, b, c, d, to_a, to_b, to_c, to_d):
+    to_a[...], to_b[...], to_c[...], to_d[...] = a[...], b[...], c[...], d[...]
 
 
 def fused_shards(
@@ -489,9 +484,8 @@
     outs = pl.pallas_call(
         written,
         out_shape=[jax.ShapeDtypeStruct(o.shape, o.dtype) for o in outs],
-        in_specs=[hbm] * 4,
-        out_specs=[hbm] * 4,
-        scratch_shapes=[pltpu.SemaphoreType.DMA((4,))],
+        in_specs=[vmem] * 4,
+        out_specs=[vmem] * 4,
         compiler_params=pltpu.CompilerParams(vmem_limit_bytes=60 * 1024 * 1024),
     )(*outs)
     return (outs[0].T, outs[1].T, outs[2].T, outs[3].reshape(-1))

time: 42 us -> 37.4 us (0.89)
  Pallas kernels: 41.2 us -> 36.6 us
    pallas_call x1, Pallas kernels: 6.16 us -> 1.54 us  [fused_shards(): pl.pallas_call(written, out_shape=[jax.ShapeDtypeStruct(o.shape, o.dtype)...]
where the time goes in v2:
time: 37.4 us; the launch traced here: 37.2 us
  Pallas kernels  36.6 us (98%)
  between operations  0.64 us (2%)
    pallas_call x1, Pallas kernels, fused_shards(): pl.pallas_call(functools.partial(fused, n_blk, n_path), out_shape=(jax.Sh...  35 us
    pallas_call x1, Pallas kernels, fused_shards(): pl.pallas_call(written, out_shape=[jax.ShapeDtypeStruct(o.shape, o.dtype)...  1.54 us

profile of v2, /device:TPU:0, one launch (start us, length us, event | category | flops | bytes accessed | tf_op | source)
XLA Modules:
  0.0 37.2 jit_solution(5721901469605480149)
XLA Ops:
  0.6 35.0 %shard_map.129 = (f32[16,1024]{1,0:T(8,128)}, f32[16,1024]{1,0:T(8,128)}, f32[16,512]{1,0:T(8,128)}, f32[1,512]{1,0:T(1,128)}) custom-call(bf16[1024,512]{1,0:T(8,128)(2,1)} %rec_hbm.1, f32[16,1024]{1,0:T(8,128)} %bitcast.9, f32[16,1024]{1,0:T(8,128)} %bitcast.10, f32[16,1024]{1,0:T(8,128)} %bitcast.11, s32[3,24]{1,0:T(4,128)} %local_hbm.1, ...), custom_call_target="tpu_custom_call" | custom-call | tf_op jit(solution)/shard_map/pallas_call | solution.py:432
  35.7 1.5 %shard_map.130 = (f32[16,1024]{1,0:T(8,128)}, f32[16,1024]{1,0:T(8,128)}, f32[16,512]{1,0:T(8,128)}, f32[1,512]{1,0:T(1,128)}) custom-call(f32[16,1024]{1,0:T(8,128)} %get-tuple-element.12.a, f32[16,1024]{1,0:T(8,128)} %get-tuple-element.13.b, f32[16,512]{1,0:T(8,128)} %get-tuple-element.14.c, f32[1,512]{1,0:T(1,128)} %get-tuple-element.15.d), custom_call_target="tpu_custom_call" | custom-call | tf_op jit(solution)/shard_map/pallas_call | solution.py:484
